TPU v7x, 512 devices: a whole 4x4x16 slice. The times are simulated.
512 devices in a mesh: dp: 16 (over x, y), expert: 32 (over z, core).
Axes of the slice: x: 4, y: 4, z: 16, core: 2. Of those that a mesh axis runs over, the one named last changes fastest.
Arguments:
- grad_out: bfloat16 [4096, 4096], P('expert', 'dp'), may hold values from -12 to 12
- route_ids: int32 [4096, 8], P('expert'), may hold values from 0 to 63, all different within a row; in each aligned block of 128 rows (0 to 127, 128 to 255, ...) at most 17 rows name the same one
- route_weights: float32 [4096, 8], P('expert'), may hold values from 0.1 to 1
- hidden_act: bfloat16 [64, 544, 1536], P('expert', 'dp'), may hold values from -0.29882812 to 0.29882812
- down_weight: bfloat16 [64, 1536, 4096], P('expert', None, 'dp'), may hold values from -0.15625 to 0.15625
- skew_param: float32 [64, 24, 64, 64], P('expert'), may hold values from -0.12 to 0.12
Outputs:
- hidden_grad: bfloat16 [64, 544, 1536], P('expert', 'dp')
- skew_grad: float32 [64, 24, 64, 64], P('expert')
Inputs may be any that keep to these rules, and one draw needn't show every extreme that they name: `route_ids`: each token names 8 different experts; within each aligned block of 128 tokens no expert is named by more than 17 of the block's choices, and in some block one expert is named by exactly 17.
All inputs are finite; a program needn't handle non-finite values.
Results may differ from a plain program's by a relative error of at most 0.02.
Values may be sent and summed in bfloat16 or wider, within the bound.
A program may use at most 128 MiB of HBM per device.

v0:
```python
import jax
import jax.numpy as jnp
from jax import lax
from jax.sharding import PartitionSpec as P

ORDER = 4


def rotation(skew_param):
    skew_mat = skew_param - jnp.swapaxes(skew_param, -1, -2)
    identity = jnp.eye(skew_mat.shape[-1], dtype=jnp.float32)
    negated = -skew_mat
    series = identity + negated
    powered = negated
    for factor_step in range(1, ORDER):
        powered = jnp.einsum(
            "...ij,...jk->...ik", powered, powered, precision=lax.Precision.HIGHEST
        )
        series = jnp.einsum(
            "...ij,...jk->...ik", series, identity + powered, precision=lax.Precision.HIGHEST
        )
    return jnp.einsum(
        "...ij,...jk->...ik", identity - skew_mat, series, precision=lax.Precision.HIGHEST
    )


def body(grad_out, route_ids, route_weights, hidden_act, down_weight, skew_param):
    token_count = grad_out.shape[0]
    feature_count = grad_out.shape[1]
    top_count = route_ids.shape[1]
    local_experts = down_weight.shape[0]
    hidden_count = down_weight.shape[1]
    block_size = skew_param.shape[-1]
    block_count = skew_param.shape[1]
    owners = lax.axis_size("expert")
    group_count = lax.axis_size("dp")
    expert_total = local_experts * owners
    slots_here = hidden_act.shape[1]
    slot_total = slots_here * group_count
    slot_depth = slot_total // owners
    flat_ids = route_ids.reshape(-1)
    onehot = (flat_ids[:, None] == jnp.arange(expert_total, dtype=jnp.int32)[None, :]).astype(
        jnp.int32
    )
    before = jnp.cumsum(onehot, axis=0) - onehot
    position = jnp.sum(before * onehot, axis=1)
    target = flat_ids // local_experts
    within = flat_ids % local_experts
    slot_index = (within * owners + target) * slot_depth + position
    sent_rows = (route_weights[:, :, None] * grad_out[:, None, :].astype(jnp.float32)).astype(
        jnp.bfloat16
    )
    sent_rows = sent_rows.reshape(token_count * top_count, feature_count)
    outgoing = jnp.zeros((local_experts * owners * slot_depth, feature_count), jnp.bfloat16)
    outgoing = (
        outgoing.at[slot_index]
        .set(sent_rows)
        .reshape(local_experts, owners, slot_depth, feature_count)
    )
    arrived = lax.all_to_all(outgoing, "expert", split_axis=1, concat_axis=1, tiled=True).reshape(
        local_experts, slot_total, feature_count
    )
    own_columns = lax.all_to_all(down_weight, "dp", split_axis=1, concat_axis=2, tiled=True)
    part_hidden = own_columns.shape[1]
    full_rows = lax.all_gather(arrived, "dp", axis=2, tiled=True)
    grouped_rows = full_rows.reshape(local_experts, slot_total, group_count, feature_count)
    grouped_weight = own_columns.reshape(local_experts, part_hidden, group_count, feature_count)
    partial_value = jnp.einsum(
        "lsgk,lfgk->lsgf", grouped_rows, grouped_weight, preferred_element_type=jnp.float32
    )
    partial_value = lax.optimization_barrier(partial_value.astype(jnp.bfloat16))
    partial_rows = jnp.sum(partial_value.astype(jnp.float32), axis=2)
    settled = lax.all_to_all(
        partial_rows.astype(jnp.bfloat16), "dp", split_axis=1, concat_axis=2, tiled=True
    ).astype(partial_rows.dtype)
    row_grad = jnp.swapaxes(settled, 0, 1)
    params_flat = skew_param.reshape(local_experts * block_count, block_size, block_size)
    share_count = params_flat.shape[0] // group_count
    own_params = lax.dynamic_slice_in_dim(
        params_flat, lax.axis_index("dp") * share_count, share_count, 0
    )
    share_rot, share_pull = jax.vjp(rotation, own_params)
    rotated = (
        lax.all_gather(share_rot.astype(jnp.bfloat16), "dp", axis=0, tiled=True)
        .astype(share_rot.dtype)
        .reshape(skew_param.shape)
    )
    grad_blocks = row_grad.reshape(slots_here, local_experts, block_count, block_size)
    hidden_grad = jnp.einsum(
        "slbc,lbac->lsba", grad_blocks, rotated, precision=lax.Precision.HIGHEST
    )
    hidden_grad = hidden_grad.astype(jnp.bfloat16).reshape(local_experts, slots_here, hidden_count)
    act_blocks = hidden_act.astype(jnp.float32).reshape(
        local_experts, slots_here, block_count, block_size
    )
    rot_part = jnp.einsum(
        "lsba,slbc->lbac", act_blocks, grad_blocks, precision=lax.Precision.HIGHEST
    )
    flat_part = rot_part.reshape(local_experts * block_count, block_size, block_size)
    own_share = lax.psum_scatter(
        flat_part.astype(jnp.bfloat16), "dp", scatter_dimension=0, tiled=True
    ).astype(jnp.float32)
    piece_grad = share_pull(own_share)[0]
    skew_grad = (
        lax.all_gather(piece_grad.astype(jnp.bfloat16), "dp", axis=0, tiled=True)
        .astype(piece_grad.dtype)
        .reshape(skew_param.shape)
    )
    return (hidden_grad, skew_grad)


def solution(mesh):
    in_specs = (
        P("expert", "dp"),
        P("expert", None),
        P("expert", None),
        P("expert", "dp", None),
        P("expert", None, "dp"),
        P("expert", None, None, None),
    )
    out_specs = (P("expert", "dp", None), P("expert", None, None, None))
    return jax.shard_map(body, mesh=mesh, in_specs=in_specs, out_specs=out_specs, check_vma=False)
```

profile of v0, /device:TPU:32, one launch (start us, length us, event | category | flops | bytes accessed | tf_op | source)
XLA Modules:
  0.0 405.2 jit_solution(10867368318475950592)
XLA Ops:
  10.0 18.0 %reduce-window.6 = s32[64,8,128]{2,1,0:T(8,128)S(1)} reduce-window(s32[64,8,128]{2,1,0:T(8,128)S(1)} %fusion.19, s32[]{:T(128)} %constant.43.clone.1), window={size=1x1x128 pad=0_0x0_0x127_0}, to_apply=%region_0.0 | reduce-window | flops 8323072 | bytes 524292 | tf_op jit(solution)/shard_map/reduce-window
  28.7 5.5 %scatter_custom_fusion = bf16[1088,256]{1,0:T(8,128)(2,1)S(1)} fusion(s32[1024]{0:T(1024)S(1)} %bitcast.108, f32[128,256]{1,0:T(8,128)S(1)} %convert_element_type.68, f32[1024]{0:T(1024)S(1)} %mul.56, bf16[]{:T(256)} %constant.45.clone.1), kind=kCustom, calls=%fused_computation.20 | custom fusion | flops 524288 | bytes 692226 | tf_op jit(solution)/shard_map/scatter | solution.py:57
  35.1 48.8 %all_to_all.38 = bf16[2,32,17,256]{3,0,2,1:T(2,128)(2,1)} all-to-all(bf16[2,32,17,256]{3,0,2,1:T(2,128)(2,1)S(1)} %copy.81), channel_id=1, replica_groups=mesh['dp'=16,'expert'=32] {'expert'}, dimensions={1} | all-to-all | bytes 1114112 | tf_op jit(solution)/shard_map/all_to_all | solution.py:60
  84.0 10.7 %copy.83 = bf16[2,1536,256]{2,0,1:T(2,128)(2,1)} copy(bf16[2,1536,256]{2,1,0:T(8,128)(2,1)S(1)} %copy-done.1) | data formatting | bytes 3145728 | tf_op args[4]
  94.7 7.2 %all-to-all-start.1 = ((bf16[2,1536,256]{2,0,1:T(2,128)(2,1)}), bf16[2,1536,256]{2,0,1:T(2,128)(2,1)S(1)}, u32[]{:S(2)}, u32[]{:S(2)}) async-start(bf16[2,1536,256]{2,0,1:T(2,128)(2,1)} %copy.83), calls=%async_computation.1 | async-start | bytes 3145728 | tf_op jit(solution)/shard_map/all_to_all | solution.py:63
  101.9 1.1 reshape.202
  102.9 1.9 copy.73
  105.4 0.9 convolution_add_fusion.6
  106.3 0.9 fusion.27
  107.2 25.3 %all-to-all-done.1 = bf16[2,1536,256]{2,0,1:T(2,128)(2,1)S(1)} async-done(((bf16[2,1536,256]{2,0,1:T(2,128)(2,1)}), bf16[2,1536,256]{2,0,1:T(2,128)(2,1)S(1)}, u32[]{:S(2)}, u32[]{:S(2)}) %all-to-all-start.1) | async-done | bytes 1572896 | tf_op jit(solution)/shard_map/all_to_all | solution.py:63
  132.7 97.5 %all-gather.2.cloned.1.call-done = bf16[2,544,4096]{2,0,1:T(2,128)(2,1)} async-done(((bf16[2,544,256]{2,0,1:T(2,128)(2,1)}), bf16[2,544,4096]{2,0,1:T(2,128)(2,1)}) %all-gather.2.cloned.1.call-update) | async-done | bytes 8912912 | tf_op jit(solution)/shard_map/all_gather | solution.py:65
  230.2 15.0 %reshape.215 = bf16[2,544,16,256]{3,2,0,1:T(8,128)(2,1)} reshape(bf16[2,544,4096]{2,0,1:T(2,128)(2,1)} %all-gather.2.cloned.1.call-done) | data formatting | bytes 17825792 | tf_op jit(solution)/shard_map/reshape | solution.py:66
  245.1 15.6 %convert_bitcast_fusion = bf16[2,544,16,96]{1,3,2,0:T(8,128)(2,1)} fusion(bf16[2,96,16,256]{3,1,2,0:T(8,128)(2,1)S(1)} %bitcast.102, bf16[2,544,16,256]{3,2,0,1:T(8,128)(2,1)} %reshape.215), kind=kOutput, calls=%fused_computation.3 | convolution fusion | flops 857309184 | bytes 13828096 | tf_op jit(solution)/shard_map/lsgk,lfgk->lsgf/dot_general | solution.py:68
  260.7 2.8 reduce_sum.25
  263.6 0.9 copy.86
  264.5 6.5 %all-to-all-start.2 = ((bf16[2,544,96]{2,0,1:T(2,128)(2,1)}), bf16[2,544,96]{2,0,1:T(2,128)(2,1)S(1)}, u32[]{:S(2)}, u32[]{:S(2)}) async-start(bf16[2,544,96]{2,0,1:T(2,128)(2,1)} %copy.86), calls=%async_computation.2 | async-start | bytes 557056 | tf_op jit(solution)/shard_map/all_to_all | solution.py:73
  271.5 8.1 %all-to-all-done.2 = bf16[2,544,96]{2,0,1:T(2,128)(2,1)S(1)} async-done(((bf16[2,544,96]{2,0,1:T(2,128)(2,1)}), bf16[2,544,96]{2,0,1:T(2,128)(2,1)S(1)}, u32[]{:S(2)}, u32[]{:S(2)}) %all-to-all-start.2) | async-done | bytes 208928 | tf_op jit(solution)/shard_map/all_to_all | solution.py:73
  280.3 1.3 convolution_convert_fusion
  282.2 22.6 %all_gather.9 = bf16[48,64,64]{2,1,0:T(8,128)(2,1)S(1)} all-gather(bf16[3,64,64]{2,1,0:T(8,128)(2,1)S(1)} %convolution_convert_fusion.2), channel_id=1, replica_groups=mesh['dp'=16,'expert'=32] {'dp'}, dimensions={0}, use_global_device_ids=true | all-gather | bytes 417792 | tf_op jit(solution)/shard_map/all_gather | solution.py:84
  305.3 0.9 reshape.201
  306.3 61.7 %reduce-scatter.4.cloned.1.call-done = bf16[3,64,64]{1,2,0:T(8,128)(2,1)} async-done(((bf16[48,64,64]{1,2,0:T(8,128)(2,1)}), bf16[3,64,64]{1,2,0:T(8,128)(2,1)}) %reduce-scatter.4.cloned.1.call-update) | async-done | bytes 24592
  368.0 1.0 fusion.31
  373.2 23.8 %all_gather.11 = bf16[48,64,64]{2,1,0:T(8,128)(2,1)S(1)} all-gather(bf16[3,64,64]{2,1,0:T(8,128)(2,1)S(1)} %fusion.20), channel_id=1, replica_groups=mesh['dp'=16,'expert'=32] {'dp'}, dimensions={0}, use_global_device_ids=true | all-gather | bytes 417792 | tf_op jit(solution)/shard_map/all_gather | solution.py:105
  397.0 1.3 convert.2
  (64 shorter events, 11.5 us)
Async XLA Ops:
  7.2 223.0 %all-gather.2.cloned.1.call-start = ((), (), s32[]{:S(2)}) async-start(), calls=%async_computation.4 | async-start | bytes 9469952 | tf_op jit(solution)/shard_map/all_gather | solution.py:65
  34.5 49.5 %copy-start.1 = (bf16[2,1536,256]{2,1,0:T(8,128)(2,1)S(1)}, bf16[2,1536,256]{2,1,0:T(8,128)(2,1)}, u32[]{:S(2)}) copy-start(bf16[2,1536,256]{2,1,0:T(8,128)(2,1)} %param.10) | copy-start | bytes 4718596
  94.7 7.2 %copy-start.4 = (bf16[2,34,1536]{2,0,1:T(2,128)(2,1)S(1)}, bf16[2,34,1536]{2,0,1:T(2,128)(2,1)}, u32[]{:S(2)}) copy-start(bf16[2,34,1536]{2,0,1:T(2,128)(2,1)} %param.9) | copy-start | bytes 626692
  94.7 37.8 %all-to-all-start.1 = ((bf16[2,1536,256]{2,0,1:T(2,128)(2,1)}), bf16[2,1536,256]{2,0,1:T(2,128)(2,1)S(1)}, u32[]{:S(2)}, u32[]{:S(2)}) async-start(bf16[2,1536,256]{2,0,1:T(2,128)(2,1)} %copy.83), calls=%async_computation.1 | async-start | bytes 3145728 | tf_op jit(solution)/shard_map/all_to_all | solution.py:63
  260.7 10.5 %copy-start.2 = (f32[3,64,64]{2,1,0:T(8,128)S(1)}, f32[3,64,64]{2,1,0:T(8,128)}, u32[]{:S(2)}) copy-start(f32[3,64,64]{2,1,0:T(8,128)} %fusion.27) | copy-start | bytes 147460
  263.6 16.8 %copy-start = (bf16[2,34,24,64]{3,2,0,1:T(8,128)(2,1)S(1)}, bf16[2,34,24,64]{3,2,0,1:T(8,128)(2,1)}, u32[]{:S(2)}) copy-start(bf16[2,34,24,64]{3,2,0,1:T(8,128)(2,1)} %reshape.202) | copy-start | bytes 626692
  264.5 15.1 %all-to-all-start.2 = ((bf16[2,544,96]{2,0,1:T(2,128)(2,1)}), bf16[2,544,96]{2,0,1:T(2,128)(2,1)S(1)}, u32[]{:S(2)}, u32[]{:S(2)}) async-start(bf16[2,544,96]{2,0,1:T(2,128)(2,1)} %copy.86), calls=%async_computation.2 | async-start | bytes 557056 | tf_op jit(solution)/shard_map/all_to_all | solution.py:73
  271.0 97.0 %reduce-scatter.4.cloned.1.call-start = ((), (), s32[]{:S(2)}) async-start(), calls=%async_computation.5 | async-start | bytes 835584
  280.0 1.7 copy-start.3
  369.9 3.0 copy-start.5
Sparse Core Ops, SparseCore 0:
  84.1 146.0 all-gather.1
  281.8 86.1 reduce-scatter.3
where the time goes:
time: 406 us; the launch traced here: 405 us
  waiting for transfers between devices  193 us (48%)
  blocking collectives  95.2 us (23%)
  local copies, waits for them, and re-layouts  34.8 us (9%)
  other arithmetic  28.9 us (7%)
  matrix products  25.3 us (6%)
  between operations  14.4 us (4%)
  starting transfers between devices  14 us (3%)
    all_gather x1, waiting for transfers between devices, body(): full_rows = lax.all_gather(arrived, 'dp', axis=2, tiled=True)  97.5 us
    unnamed x3, waiting for transfers between devices  61.8 us
    all_to_all x1, blocking collectives, body(): lax.all_to_all(outgoing, 'expert', split_axis=1, concat_axis=1, tiled=True)  48.8 us
    all_to_all x1, waiting for transfers between devices, body(): lax.all_to_all(down_weight, 'dp', split_axis=1, concat_axis=2, tiled=True)  25.3 us
    all_gather x1, blocking collectives, body(): lax.all_gather(piece_grad.astype(jnp.bfloat16), 'dp', axis=0, tiled=True)  23.8 us
    all_gather x1, blocking collectives, body(): lax.all_gather(share_rot.astype(jnp.bfloat16), 'dp', axis=0, tiled=True)  22.6 us
    another operation x3, other arithmetic  18.2 us
    dot_general x1, matrix products, body(): jnp.einsum('lsgk,lfgk->lsgf', grouped_rows, grouped_weight, preferred_ele...  15.6 us
  transfers between devices with their start and end apart: 4, of which 4 were waited for; matrix products, arithmetic and copies ran while one was open for 5% of the time, Pallas kernels for 0%

commit v1 on v0

v1 whole, which is shorter than its diff:
```python
import functools

import jax
import jax.numpy as jnp
from jax import lax
from jax.experimental import pallas as pl
from jax.experimental.pallas import tpu as pltpu
from jax.sharding import PartitionSpec as P

F32 = jnp.float32
BF16 = jnp.bfloat16
MESH = pl.DeviceIdType.MESH
MOST = 17
PER = 4
HEAD = 40
DEEP = 48


def dot(a, b, dims=((1,), (0,))):
    return lax.dot_general(a, b, (dims, ((), ())), preferred_element_type=F32)


def halves(value):
    high = value.astype(BF16)
    return high, (value - high.astype(F32)).astype(BF16)


def spread(slab, mask):
    return jnp.concatenate([slab] * PER, axis=0) * mask


def fold(square):
    size = square.shape[0] // PER
    total = square[:size]
    for band in range(1, PER):
        total = total + square[band * size : (band + 1) * size]
    return total


def both(slab, mask):
    high, low = halves(slab)
    return spread(high, mask), spread(low, mask)


def times(left, right):
    rows = left.shape[0]
    high, low = halves(left)
    first = dot(jnp.concatenate([high, low], axis=0), right[0])
    return first[:rows] + first[rows:] + dot(high, right[1])


def negated_skew(stack, mask):
    square = spread(stack.T, mask)
    return fold(square - square.T)


def kernel(
    side, depth, groups,
    ids_ref, wts_ref, grad_ref, act_ref, w_ref, skew_ref,
    hid_ref, skg_ref,
    gath, part, rxa, rxb, mida, midb, tra, trb, rgs, rotm, rotp, rotrx, pull, maskf, maskb, bys, lefts, values,
    s_right, s_left, s_sib, r_gath, s_a, s_b, r_a, r_b, s_ma, s_mb, r_ma, r_mb,
    s_rot, r_rot, s_pull, r_pull,
):
    n_dp = side * side
    dp = lax.axis_index("dp")
    ex = lax.axis_index("expert")
    x, y = dp // side, dp % side
    z, core = ex // 2, ex % 2
    hidden = w_ref.shape[1]
    half = hidden // 2
    size = skew_ref.shape[1] // PER
    per_expert = groups // 2
    right = lax.rem(z + 1, depth) * 2 + core
    left = lax.rem(z + depth - 1, depth) * 2 + core
    sibling = z * 2 + (1 - core)

    def copy(src, dst, send, recv, to_dp, to_ex):
        return pltpu.make_async_remote_copy(
            src_ref=src, dst_ref=dst, send_sem=send, recv_sem=recv,
            device_id=(to_dp, to_ex), device_id_type=MESH,
        )

    barrier = pltpu.get_barrier_semaphore()
    for peer in (right, left, sibling):
        pl.semaphore_signal(barrier, inc=1, device_id=(dp, peer), device_id_type=MESH)

    def greet(step, carry):
        pl.semaphore_signal(
            barrier, inc=1, device_id=(lax.rem(dp + step, n_dp), ex), device_id_type=MESH
        )
        return carry

    lax.fori_loop(1, n_dp, greet, 0)

    tokens = grad_ref.shape[0]
    own = ex
    gath[own, 0:tokens, :] = grad_ref[...]
    weight = wts_ref[...]
    w1 = weight.astype(BF16).astype(F32)
    w2 = (weight - w1).astype(BF16).astype(F32)
    w3 = weight - w1 - w2
    info = jnp.concatenate(
        [
            jnp.concatenate([ids_ref[...].astype(F32), w1], axis=1),
            jnp.concatenate([w2, w3], axis=1),
        ],
        axis=0,
    )
    gath[own, tokens : tokens + 16, :] = info.astype(BF16)

    row_i = lax.broadcasted_iota(jnp.int32, (PER * size, PER * size), 0) // size
    col_i = lax.broadcasted_iota(jnp.int32, (PER * size, PER * size), 1) // size
    maskf[...] = (row_i == col_i).astype(F32)
    maskb[...] = (row_i == col_i).astype(F32).astype(BF16)

    pl.semaphore_wait(barrier, n_dp - 1 + 3)

    def go_right(block):
        return copy(gath.at[block], gath.at[block], s_right.at[block // 2], r_gath.at[block], dp, right)

    def go_left(block):
        return copy(gath.at[block], gath.at[block], s_left.at[block // 2], r_gath.at[block], dp, left)

    def go_across(block):
        return copy(gath.at[block], gath.at[block], s_sib.at[block // 2], r_gath.at[block], dp, sibling)

    go_right(own).start()
    go_left(own).start()
    go_across(own).start()

    upper = (
        lax.broadcasted_iota(jnp.int32, (tokens, tokens), 0)
        < lax.broadcasted_iota(jnp.int32, (tokens, tokens), 1)
    ).astype(F32).astype(BF16)

    def rows_of(root):
        hits, heavy = [], []
        for turn in range(2):
            data = gath[root * 2 + turn, tokens : tokens + 16, :].astype(F32)
            named = data[0:8, 0:tokens]
            weights = data[0:8, tokens:] + data[8:16, 0:tokens] + data[8:16, tokens:]
            for local in range(2):
                hit = (named == (ex * 2 + local).astype(F32)).astype(F32)
                hits.append(jnp.sum(hit, axis=0, keepdims=True))
                heavy.append(jnp.sum(hit * weights, axis=0, keepdims=True))
        taken = jnp.concatenate(hits + [jnp.zeros((4, tokens), F32)], axis=0)
        rank = dot(taken.astype(BF16), upper)
        place = lax.broadcasted_iota(jnp.int32, (HEAD, tokens), 0).astype(F32)
        picks, scales = [], []
        for local in range(2):
            chosen, scale = [], None
            for turn in range(2):
                at = turn * 2 + local
                slot = jnp.where(
                    taken[at : at + 1] > 0, rank[at : at + 1] + float(turn * MOST), -1.0
                )
                equal = place == slot
                chosen.append(equal.astype(F32))
                term = jnp.sum(jnp.where(equal, heavy[at], 0.0), axis=1, keepdims=True)
                scale = term if scale is None else scale + term
            picks.append(jnp.concatenate(chosen, axis=1))
            scales.append(scale)
        pick = jnp.concatenate(picks, axis=0).astype(BF16)
        rows = jnp.concatenate(
            [gath[root * 2, 0:tokens, :], gath[root * 2 + 1, 0:tokens, :]], axis=0
        )
        routed = dot(pick, rows)
        return [routed[local * HEAD : (local + 1) * HEAD] * scales[local] for local in range(2)]

    def process(roots):
        found = [rows_of(root) for root in roots]
        sums = []
        for local in range(2):
            lhs = jnp.concatenate([f[local] for f in found], axis=0).astype(BF16)
            sums.append(dot(lhs, w_ref[local], ((1,), (1,))))
        for n, root in enumerate(roots):
            for which in range(2):
                part[root, which] = jnp.concatenate(
                    [
                        s[n * HEAD : (n + 1) * HEAD, which * half : (which + 1) * half]
                        for s in sums
                    ],
                    axis=0,
                ).astype(BF16)
            jx, jy = root // side, root % side

            @pl.when(jy != y)
            def _():
                first_a(root).start()

            @pl.when(jx != x)
            def _():
                first_b(root).start()

    def first_a(root):
        jx, jy = root // side, root % side
        off = lax.rem(jy - y + side, side)
        slot = jnp.maximum(off - 1, 0)
        return copy(part.at[root, 0], rxa.at[jx, slot], s_a.at[root], r_a.at[jx, slot], x * side + jy, ex)

    def first_b(root):
        jx, jy = root // side, root % side
        off = lax.rem(jx - x + side, side)
        slot = jnp.maximum(off - 1, 0)
        return copy(part.at[root, 1], rxb.at[jy, slot], s_b.at[root], r_b.at[jy, slot], jx * side + y, ex)

    def arrived(block):
        go_right(block).wait_recv()

    arrived(sibling)
    process([z])

    def ring(step, carry):
        low = lax.rem(z - step + depth, depth)
        high = lax.rem(z + step, depth)
        arrived(low * 2 + core)
        go_right(low * 2 + core).start()
        arrived(high * 2 + core)

        @pl.when(step < depth // 2 - 1)
        def _():
            go_left(high * 2 + core).start()

        go_across(low * 2 + core).start()
        go_across(high * 2 + core).start()
        arrived(low * 2 + 1 - core)
        arrived(high * 2 + 1 - core)
        process([low, high])
        return carry

    lax.fori_loop(1, depth // 2, ring, 0)
    far = lax.rem(z + depth // 2, depth)
    arrived(far * 2 + core)
    go_across(far * 2 + core).start()
    arrived(far * 2 + 1 - core)
    process([far])

    eye = (
        lax.broadcasted_iota(jnp.int32, (size, PER * size), 0)
        == lax.rem(lax.broadcasted_iota(jnp.int32, (size, PER * size), 1), size)
    ).astype(F32)

    def turn(group, carry):
        mask = maskb[...]
        first = negated_skew(skew_ref[group], maskf[...])
        by_first = both(first, mask)
        second = times(first, by_first)
        series = eye + first
        pair = times(jnp.concatenate([second, series], axis=0), both(second, mask))
        fourth, series = pair[:size], series + pair[size:]
        pair = times(jnp.concatenate([fourth, series], axis=0), both(fourth, mask))
        eighth, series = pair[:size], series + pair[size:]
        series = series + times(series, both(eighth, mask))
        result = series + times(series, by_first)
        rotm[group] = spread(result.astype(BF16), mask)
        return carry

    lax.fori_loop(0, groups, turn, 0)

    def prepare():
        mask = maskb[...]
        given = -negated_skew(skew_ref[jnp.minimum(dp, groups - 1)], maskf[...])

        def keep(which, slab):
            right = both(slab, mask)
            bys[which] = right[0]
            return right

        second = times(given, keep(0, given))
        one = eye + given
        pair = times(jnp.concatenate([second, one], axis=0), keep(1, second))
        fourth, two = pair[:size], one + pair[size:]
        pair = times(jnp.concatenate([fourth, two], axis=0), keep(2, fourth))
        eighth, three = pair[:size], two + pair[size:]
        keep(4, three + times(three, keep(3, eighth)))
        for which, slab in enumerate((given, second, one, fourth, two, three)):
            lefts[which] = slab.astype(BF16)

    prepare()

    def gather_a(jx, carry):
        root = jx * side + y
        total = part[root, 0].astype(F32)
        for slot in range(side - 1):
            copy(part.at[root, 0], rxa.at[jx, slot], s_a.at[root], r_a.at[jx, slot], dp, ex).wait_recv()
            total = total + rxa[jx, slot].astype(F32)
        mida[jx] = total.astype(BF16)

        @pl.when(jx != x)
        def _():
            second_a(jx).start()

        return carry

    def second_a(jx):
        slot = jnp.maximum(lax.rem(jx - x + side, side) - 1, 0)
        return copy(mida.at[jx], tra.at[slot], s_ma.at[jx], r_ma.at[slot], jx * side + y, ex)

    def gather_b(jy, carry):
        root = x * side + jy
        total = part[root, 1].astype(F32)
        for slot in range(side - 1):
            copy(part.at[root, 1], rxb.at[jy, slot], s_b.at[root], r_b.at[jy, slot], dp, ex).wait_recv()
            total = total + rxb[jy, slot].astype(F32)
        midb[jy] = total.astype(BF16)

        @pl.when(jy != y)
        def _():
            second_b(jy).start()

        return carry

    def second_b(jy):
        slot = jnp.maximum(lax.rem(jy - y + side, side) - 1, 0)
        return copy(midb.at[jy], trb.at[slot], s_mb.at[jy], r_mb.at[slot], x * side + jy, ex)

    def gather_both(step, carry):
        gather_a(step, 0)
        gather_b(step, 0)
        return carry

    lax.fori_loop(0, side, gather_both, 0)

    for which, (mid, at, tr, s_m, r_m) in enumerate(((mida, x, tra, s_ma, r_ma), (midb, y, trb, s_mb, r_mb))):
        total = mid[at].astype(F32)
        for slot in range(side - 1):
            copy(mid.at[0], tr.at[slot], s_m.at[0], r_m.at[slot], dp, ex).wait_recv()
            total = total + tr[slot].astype(F32)
        for local in range(2):
            rgs[local, :, which * half : (which + 1) * half] = jnp.concatenate(
                [total[local * HEAD : (local + 1) * HEAD], jnp.zeros((DEEP - HEAD, half), F32)], axis=0
            ).astype(BF16)

    def lanes_of(group):
        return pl.ds(pl.multiple_of((group % per_expert) * PER * size, PER * size), PER * size)

    def rot_copy(group):
        return copy(rotp.at[group], rotrx.at[dp], s_rot.at[group], r_rot.at[dp], group, ex)

    def grads(group, carry):
        local, lanes = group // per_expert, lanes_of(group)
        square = dot(act_ref[local, :, lanes], rgs[local, :, lanes], ((0,), (0,)))
        rotp[group] = fold(square * maskf[...]).astype(BF16)

        @pl.when(group != dp)
        def _():
            rot_copy(group).start()

        return carry

    lax.fori_loop(0, groups, grads, 0)

    def hide(group, carry):
        local, lanes = group // per_expert, lanes_of(group)
        hid_ref[local, :, lanes] = dot(rgs[local, :, lanes], rotm[group], ((1,), (1,))).astype(BF16)
        return carry

    lax.fori_loop(0, groups, hide, 0)

    def pull_copy(owner, peer):
        return copy(pull.at[owner], pull.at[owner], s_pull.at[peer], r_pull.at[owner], peer, ex)

    @pl.when(dp < groups)
    def _():
        mask = maskb[...]

        def add(step, total):
            source = lax.rem(dp + step, n_dp)
            copy(rotp.at[0], rotrx.at[source], s_rot.at[0], r_rot.at[source], dp, ex).wait_recv()
            return total + rotrx[source].astype(F32)

        change = lax.fori_loop(1, n_dp, add, rotp[dp].astype(F32))
        change_b = change.astype(BF16)

        none = dp // n_dp

        def put(at, left, right):
            rows = left.shape[0] // size
            values[at : at + rows] = dot(left, right).reshape(rows, size, PER * size)
            return [values[at + row + none] for row in range(rows)]

        def rows_at(first, count):
            return lefts[first : first + count].reshape(count * size, PER * size)

        (front,) = put(0, rows_at(0, 1), spread(change_b, mask))
        (back,) = put(1, change_b, bys[0])
        change2 = (front + back).astype(BF16)
        front, lower = put(2, rows_at(1, 2), spread(change2, mask))
        (back,) = put(4, change2, bys[1])
        change4 = (front + back).astype(BF16)
        (back,) = put(5, change_b, bys[1])
        two_change = change + back + lower
        front, lower = put(6, rows_at(3, 2), spread(change4, mask))
        (back,) = put(8, change4, bys[2])
        change8 = (front + back).astype(BF16)
        (back,) = put(9, two_change.astype(BF16), bys[2])
        three_change = two_change + back + lower
        (lower,) = put(10, rows_at(5, 1), spread(change8, mask))
        (back,) = put(11, three_change.astype(BF16), bys[3])
        four_change = three_change + back + lower
        (front,) = put(12, rows_at(0, 1), spread(four_change.astype(BF16), mask))
        (back,) = put(13, change_b, bys[4])
        result = front + four_change + back
        square = spread(result, maskf[...])
        pull[dp] = fold(square.T - square).astype(BF16)

        def tell(step, carry):
            pull_copy(dp, lax.rem(dp + step, n_dp)).start()
            return carry

        lax.fori_loop(1, n_dp, tell, 0)

    def write(group, carry):
        @pl.when(group != dp)
        def _():
            pull_copy(group, dp).wait_recv()

        skg_ref[group] = -(pull[group].astype(F32).T)
        return carry

    lax.fori_loop(0, groups, write, 0)

    def left_ring(step, carry):
        go_across(lax.rem(z + step, depth) * 2 + core).wait_send()

        @pl.when(step < depth // 2)
        def _():
            go_right(lax.rem(z - step + depth, depth) * 2 + core).wait_send()

        @pl.when(step < depth // 2 - 1)
        def _():
            go_left(lax.rem(z + step, depth) * 2 + core).wait_send()

        return carry

    lax.fori_loop(0, depth, left_ring, 0)

    def left_first(root, carry):
        @pl.when(root % side != y)
        def _():
            first_a(root).wait_send()

        @pl.when(root // side != x)
        def _():
            first_b(root).wait_send()

        return carry

    lax.fori_loop(0, n_dp, left_first, 0)

    def left_second(step, carry):
        @pl.when(step != x)
        def _():
            second_a(step).wait_send()

        @pl.when(step != y)
        def _():
            second_b(step).wait_send()

        return carry

    lax.fori_loop(0, side, left_second, 0)

    def left_rot(group, carry):
        @pl.when(group != dp)
        def _():
            rot_copy(group).wait_send()

        return carry

    lax.fori_loop(0, groups, left_rot, 0)

    @pl.when(dp < groups)
    def _():
        def told(step, carry):
            pull_copy(dp, lax.rem(dp + step, n_dp)).wait_send()
            return carry

        lax.fori_loop(1, n_dp, told, 0)


def body(side, depth, grad_out, route_ids, route_weights, hidden_act, down_weight, skew_param):
    tokens, feat = grad_out.shape
    local, slots_here, hidden = hidden_act.shape
    blocks, size = skew_param.shape[1], skew_param.shape[2]
    groups = local * blocks // PER
    n_dp = side * side
    half = hidden // 2
    wide = PER * size
    act = jnp.pad(hidden_act, ((0, 0), (0, DEEP - slots_here), (0, 0)))
    vmem = pl.BlockSpec(memory_space=pltpu.VMEM)
    dma = pltpu.SemaphoreType.DMA
    hid, skg = pl.pallas_call(
        functools.partial(kernel, side, depth, groups),
        out_shape=(
            jax.ShapeDtypeStruct((local, DEEP, hidden), BF16),
            jax.ShapeDtypeStruct((groups, wide, size), F32),
        ),
        in_specs=[vmem] * 6,
        out_specs=(vmem, vmem),
        scratch_shapes=[
            pltpu.VMEM((2 * depth, tokens + 16, feat), BF16),
            pltpu.VMEM((n_dp, 2, 2 * HEAD, half), BF16),
            pltpu.VMEM((side, side - 1, 2 * HEAD, half), BF16),
            pltpu.VMEM((side, side - 1, 2 * HEAD, half), BF16),
            pltpu.VMEM((side, 2 * HEAD, half), BF16),
            pltpu.VMEM((side, 2 * HEAD, half), BF16),
            pltpu.VMEM((side - 1, 2 * HEAD, half), BF16),
            pltpu.VMEM((side - 1, 2 * HEAD, half), BF16),
            pltpu.VMEM((local, DEEP, hidden), BF16),
            pltpu.VMEM((groups, wide, wide), BF16),
            pltpu.VMEM((groups, size, wide), BF16),
            pltpu.VMEM((n_dp, size, wide), BF16),
            pltpu.VMEM((groups, size, wide), BF16),
            pltpu.VMEM((wide, wide), F32),
            pltpu.VMEM((wide, wide), BF16),
            pltpu.VMEM((5, wide, wide), BF16),
            pltpu.VMEM((6, size, wide), BF16),
            pltpu.VMEM((14, size, wide), F32),
            dma((depth,)), dma((depth,)), dma((depth,)), dma((2 * depth,)),
            dma((n_dp,)), dma((n_dp,)), dma((side, side - 1)), dma((side, side - 1)),
            dma((side,)), dma((side,)), dma((side - 1,)), dma((side - 1,)),
            dma((groups,)), dma((n_dp,)), dma((n_dp,)), dma((groups,)),
        ],
        compiler_params=pltpu.CompilerParams(
            collective_id=0, has_side_effects=True, vmem_limit_bytes=50 * 1024 * 1024
        ),
    )(
        route_ids.T, route_weights.T, grad_out, act, down_weight,
        skew_param.reshape(groups, wide, size),
    )
    return hid[:, :slots_here], skg.reshape(skew_param.shape)


def solution(mesh):
    in_specs = (
        P("expert", "dp"),
        P("expert", None),
        P("expert", None),
        P("expert", "dp", None),
        P("expert", None, "dp"),
        P("expert", None, None, None),
    )
    out_specs = (P("expert", "dp", None), P("expert", None, None, None))
    side = {4: 2, 16: 4}[mesh.shape["dp"]]
    return jax.shard_map(
        functools.partial(body, side, mesh.shape["expert"] // 2),
        mesh=mesh, in_specs=in_specs, out_specs=out_specs, check_vma=False,
    )
```

time: 406 us -> 101 us (0.25)
  the two profiles are of different devices: /device:TPU:32 before, /device:TPU:8 now
where the time goes in v1:
time: 101 us; the launch traced here: 100 us
  Pallas kernels  93 us (92%)
  local copies, waits for them, and re-layouts  6.6 us (7%)
    pallas_call x1, Pallas kernels, body(): pl.pallas_call(functools.partial(kernel, side, depth, groups), out_shape=...  93 us
    unnamed x11, local copies, waits for them, and re-layouts  6.56 us

profile of v1, /device:TPU:8, one launch (start us, length us, event | category | flops | bytes accessed | tf_op | source)
XLA Modules:
  0.0 100.3 jit_solution(8868607391654129191)
XLA Ops:
  0.6 1.0 copy.8
  1.6 0.0 copy-start
  1.6 1.4 %copy-done = bf16[2,1536,256]{2,1,0:T(8,128)(2,1)S(1)} copy-done((bf16[2,1536,256]{2,1,0:T(8,128)(2,1)S(1)}, bf16[2,1536,256]{2,1,0:T(8,128)(2,1)}, u32[]{:S(2)}) %copy-start) | copy-done | bytes 1572888
  3.0 0.0 copy-start.1
  3.0 0.8 copy-done.1
  3.9 0.0 copy-start.2
  3.9 0.7 copy-done.2
  4.6 0.0 copy-start.3
  4.6 0.7 copy-done.3
  5.2 93.0 %shard_map.77 = (bf16[2,48,1536]{2,1,0:T(8,128)(2,1)S(1)}, f32[12,256,64]{2,1,0:T(8,128)S(1)}) custom-call(s32[8,128]{1,0:T(8,128)S(1)} %bitcast.5, f32[8,128]{1,0:T(8,128)S(1)} %bitcast.6, bf16[128,256]{1,0:T(8,128)(2,1)S(1)} %copy-done.1, bf16[2,48,1536]{2,1,0:T(8,128)(2,1)S(1)} %pad.4.act_ref, bf16[2,1536,256]{2,1,0:T(8,128)(2,1)S(1)} %copy-done, ...), custom_call_target="tpu_custom_call" | custom-call | tf_op jit(solution)/shard_map/pallas_call | solution.py:494
  98.3 0.8 copy.9
  99.2 1.1 %copy.11 = f32[2,24,64,64]{3,2,1,0:T(8,128)} copy(f32[2,24,64,64]{3,2,1,0:T(8,128)S(1)} %bitcast.4) | data formatting | bytes 1572864
  (2 shorter events, 0.0 us)
Async XLA Ops:
  1.6 1.4 %copy-start = (bf16[2,1536,256]{2,1,0:T(8,128)(2,1)S(1)}, bf16[2,1536,256]{2,1,0:T(8,128)(2,1)}, u32[]{:S(2)}) copy-start(bf16[2,1536,256]{2,1,0:T(8,128)(2,1)} %w_ref.1) | copy-start | bytes 4718596
  3.0 0.8 copy-start.1
  3.9 0.7 copy-start.2
  4.6 0.7 copy-start.3

commit v2 on v1

--- a/solution.py
+++ b/solution.py
@@ -56,10 +56,11 @@
 
 def kernel(
     side, depth, groups,
-    ids_ref, wts_ref, grad_ref, act_ref, w_ref, skew_ref,
+    ids_in, wts_in, grad_in, act_in, w_in, skew_in,
     hid_ref, skg_ref,
+    ids_ref, wts_ref, act_ref, w_ref, skew_ref,
     gath, part, rxa, rxb, mida, midb, tra, trb, rgs, rotm, rotp, rotrx, pull, maskf, maskb, bys, lefts, values,
-    s_right, s_left, s_sib, r_gath, s_a, s_b, r_a, r_b, s_ma, s_mb, r_ma, r_mb,
+    s_far, s_near, s_two, s_sib, r_gath, s_in, s_a, s_b, r_a, r_b, s_ma, s_mb, r_ma, r_mb,
     s_rot, r_rot, s_pull, r_pull,
 ):
     n_dp = side * side
@@ -71,8 +72,12 @@
     half = hidden // 2
     size = skew_ref.shape[1] // PER
     per_expert = groups // 2
-    right = lax.rem(z + 1, depth) * 2 + core
-    left = lax.rem(z + depth - 1, depth) * 2 + core
+    quarter = depth // 4
+
+    def at_z(step):
+        chip = lax.rem(z + step + depth, depth)
+        return chip, chip * 2 + core
+
     sibling = z * 2 + (1 - core)
 
     def copy(src, dst, send, recv, to_dp, to_ex):
@@ -81,8 +86,21 @@
             device_id=(to_dp, to_ex), device_id_type=MESH,
         )
 
+    own = ex
+    tokens = grad_in.shape[0]
+    loads = [
+        pltpu.make_async_copy(src, dst, s_in.at[n])
+        for n, (src, dst) in enumerate((
+            (ids_in, ids_ref), (wts_in, wts_ref), (grad_in, gath.at[own, pl.ds(0, tokens)]),
+            (w_in, w_ref), (skew_in, skew_ref), (act_in, act_ref),
+        ))
+    ]
+    for load in loads:
+        load.start()
+
     barrier = pltpu.get_barrier_semaphore()
-    for peer in (right, left, sibling):
+    near_steps = sorted({1, depth - 1, 2, depth - 2, quarter, depth - quarter, 2 * quarter})
+    for peer in [sibling] + [at_z(step)[1] for step in near_steps]:
         pl.semaphore_signal(barrier, inc=1, device_id=(dp, peer), device_id_type=MESH)
 
     def greet(step, carry):
@@ -93,9 +111,8 @@
 
     lax.fori_loop(1, n_dp, greet, 0)
 
-    tokens = grad_ref.shape[0]
-    own = ex
-    gath[own, 0:tokens, :] = grad_ref[...]
+    for load in loads[:2]:
+        load.wait()
     weight = wts_ref[...]
     w1 = weight.astype(BF16).astype(F32)
     w2 = (weight - w1).astype(BF16).astype(F32)
@@ -114,20 +131,36 @@
     maskf[...] = (row_i == col_i).astype(F32)
     maskb[...] = (row_i == col_i).astype(F32).astype(BF16)
 
-    pl.semaphore_wait(barrier, n_dp - 1 + 3)
-
-    def go_right(block):
-        return copy(gath.at[block], gath.at[block], s_right.at[block // 2], r_gath.at[block], dp, right)
-
-    def go_left(block):
-        return copy(gath.at[block], gath.at[block], s_left.at[block // 2], r_gath.at[block], dp, left)
-
-    def go_across(block):
-        return copy(gath.at[block], gath.at[block], s_sib.at[block // 2], r_gath.at[block], dp, sibling)
-
-    go_right(own).start()
-    go_left(own).start()
-    go_across(own).start()
+    loads[2].wait()
+    pl.semaphore_wait(barrier, n_dp - 1 + 1 + len(near_steps))
+
+    turns = (0, quarter, depth - quarter, 2 * quarter)
+
+    def send(block, sem, to_ex):
+        return copy(gath.at[block], gath.at[block], sem, r_gath.at[block], dp, to_ex)
+
+    def go_far(n):
+        return send(own, s_far.at[n], at_z(turns[n + 1])[1])
+
+    def go_near(n, down):
+        return send(at_z(turns[n])[1], s_near.at[n, down], at_z(-1 if down else 1)[1])
+
+    def go_two(n):
+        which, step = ((0, 2), (0, -2), (2, 2), (1, -2))[n]
+        return send(at_z(turns[which])[1], s_two.at[n], at_z(step)[1])
+
+    def go_across(chip):
+        block = chip * 2 + core
+        return send(block, s_sib.at[chip], sibling)
+
+    for n in range(2):
+        go_far(n).start()
+    go_near(0, 0).start()
+    go_near(0, 1).start()
+    go_far(2).start()
+    go_two(0).start()
+    go_two(1).start()
+    go_across(z).start()
 
     upper = (
         lax.broadcasted_iota(jnp.int32, (tokens, tokens), 0)
@@ -206,35 +239,51 @@
         return copy(part.at[root, 1], rxb.at[jy, slot], s_b.at[root], r_b.at[jy, slot], jx * side + y, ex)
 
     def arrived(block):
-        go_right(block).wait_recv()
+        send(block, s_sib.at[0], sibling).wait_recv()
+
+    def take(roots):
+        for root in roots:
+            go_across(root).start()
+        for root in roots:
+            arrived(root * 2 + 1 - core)
+        process(roots)
 
     arrived(sibling)
+    loads[3].wait()
     process([z])
-
-    def ring(step, carry):
-        low = lax.rem(z - step + depth, depth)
-        high = lax.rem(z + step, depth)
-        arrived(low * 2 + core)
-        go_right(low * 2 + core).start()
-        arrived(high * 2 + core)
-
-        @pl.when(step < depth // 2 - 1)
-        def _():
-            go_left(high * 2 + core).start()
-
-        go_across(low * 2 + core).start()
-        go_across(high * 2 + core).start()
-        arrived(low * 2 + 1 - core)
-        arrived(high * 2 + 1 - core)
-        process([low, high])
-        return carry
-
-    lax.fori_loop(1, depth // 2, ring, 0)
-    far = lax.rem(z + depth // 2, depth)
-    arrived(far * 2 + core)
-    go_across(far * 2 + core).start()
-    arrived(far * 2 + 1 - core)
-    process([far])
+    ahead, behind, far = (at_z(turns[n]) for n in (1, 2, 3))
+    arrived(ahead[1])
+    go_near(1, 0).start()
+    go_near(1, 1).start()
+    go_two(3).start()
+    arrived(behind[1])
+    go_near(2, 0).start()
+    go_near(2, 1).start()
+    go_two(2).start()
+    take([ahead[0], behind[0]])
+    arrived(far[1])
+    go_near(3, 0).start()
+    go_near(3, 1).start()
+    take([far[0]])
+
+    def beside(step, carry):
+        low, high = at_z(step * quarter - 1), at_z(step * quarter + 1)
+        arrived(low[1])
+        arrived(high[1])
+        take([low[0], high[0]])
+        return carry
+
+    def opposite(step, carry):
+        low, high = at_z(step * quarter + 2), at_z((step + 2) * quarter + 2)
+        arrived(low[1])
+        arrived(high[1])
+        take([low[0], high[0]])
+        return carry
+
+    lax.fori_loop(0, 4, beside, 0)
+    lax.fori_loop(0, 2, opposite, 0)
+    loads[4].wait()
+    loads[5].wait()
 
     eye = (
         lax.broadcasted_iota(jnp.int32, (size, PER * size), 0)
@@ -421,20 +470,18 @@
 
     lax.fori_loop(0, groups, write, 0)
 
-    def left_ring(step, carry):
-        go_across(lax.rem(z + step, depth) * 2 + core).wait_send()
-
-        @pl.when(step < depth // 2)
-        def _():
-            go_right(lax.rem(z - step + depth, depth) * 2 + core).wait_send()
-
-        @pl.when(step < depth // 2 - 1)
-        def _():
-            go_left(lax.rem(z + step, depth) * 2 + core).wait_send()
-
-        return carry
-
-    lax.fori_loop(0, depth, left_ring, 0)
+    for n in range(3):
+        go_far(n).wait_send()
+    for n in range(4):
+        go_near(n, 0).wait_send()
+        go_near(n, 1).wait_send()
+        go_two(n).wait_send()
+
+    def left_across(chip, carry):
+        go_across(chip).wait_send()
+        return carry
+
+    lax.fori_loop(0, depth, left_across, 0)
 
     def left_first(root, carry):
         @pl.when(root % side != y)
@@ -497,9 +544,14 @@
             jax.ShapeDtypeStruct((local, DEEP, hidden), BF16),
             jax.ShapeDtypeStruct((groups, wide, size), F32),
         ),
-        in_specs=[vmem] * 6,
+        in_specs=[pl.BlockSpec(memory_space=pltpu.HBM)] * 6,
         out_specs=(vmem, vmem),
         scratch_shapes=[
+            pltpu.VMEM((8, tokens), jnp.int32),
+            pltpu.VMEM((8, tokens), F32),
+            pltpu.VMEM((local, DEEP, hidden), BF16),
+            pltpu.VMEM((local, hidden, feat), BF16),
+            pltpu.VMEM((groups, wide, size), F32),
             pltpu.VMEM((2 * depth, tokens + 16, feat), BF16),
             pltpu.VMEM((n_dp, 2, 2 * HEAD, half), BF16),
             pltpu.VMEM((side, side - 1, 2 * HEAD, half), BF16),
@@ -518,13 +570,13 @@
             pltpu.VMEM((5, wide, wide), BF16),
             pltpu.VMEM((6, size, wide), BF16),
             pltpu.VMEM((14, size, wide), F32),
-            dma((depth,)), dma((depth,)), dma((depth,)), dma((2 * depth,)),
+            dma((3,)), dma((4, 2)), dma((4,)), dma((depth,)), dma((2 * depth,)), dma((6,)),
             dma((n_dp,)), dma((n_dp,)), dma((side, side - 1)), dma((side, side - 1)),
             dma((side,)), dma((side,)), dma((side - 1,)), dma((side - 1,)),
             dma((groups,)), dma((n_dp,)), dma((n_dp,)), dma((groups,)),
         ],
         compiler_params=pltpu.CompilerParams(
-            collective_id=0, has_side_effects=True, vmem_limit_bytes=50 * 1024 * 1024
+            collective_id=0, has_side_effects=True, vmem_limit_bytes=63 * 1024 * 1024
         ),
     )(
         route_ids.T, route_weights.T, grad_out, act, down_weight,

time: 101 us -> 113 us (1.12)
  the two profiles are of different devices: /device:TPU:8 before, /device:TPU:64 now
where the time goes in v2:
time: 113 us
  Pallas kernels  106 us (94%)
  local copies, waits for them, and re-layouts  6.23 us (6%)
    pallas_call x1, Pallas kernels, body(): pl.pallas_call(functools.partial(kernel, side, depth, groups), out_shape=...  106 us
    unnamed x3, local copies, waits for them, and re-layouts  4.53 us

profile of v2, /device:TPU:64, one launch (start us, length us, event | category | flops | bytes accessed | tf_op | source)
XLA Modules:
  0.0 112.8 jit_solution(10827952505761803148)
XLA Ops:
  0.6 1.0 copy.8
  1.6 0.7 pad.4.act_in
  2.3 105.9 %shard_map.77 = (bf16[2,48,1536]{2,1,0:T(8,128)(2,1)}, f32[12,256,64]{2,1,0:T(8,128)}) custom-call(s32[8,128]{1,0:T(8,128)} %bitcast.6, f32[8,128]{1,0:T(8,128)} %bitcast.7, bf16[128,256]{1,0:T(8,128)(2,1)} %grad_in.1, bf16[2,48,1536]{2,1,0:T(8,128)(2,1)} %pad.4.act_in, bf16[2,1536,256]{2,1,0:T(8,128)(2,1)} %w_in.1, f32[12,256,64]{2,1,0:T(8,128)} %bitcast.4), custom_call_target="tpu_custom_call" | custom-call | tf_op jit(solution)/shard_map/pallas_call | solution.py:541
  108.2 1.0 slice.3
  109.2 0.8 copy.9
  110.0 2.7 %copy.11 = f32[2,24,64,64]{3,2,1,0:T(8,128)} copy(f32[2,24,64,64]{3,2,1,0:T(8,128)} %bitcast.5) | data formatting | bytes 1572864

commit v3 on v1

--- a/solution.py
+++ b/solution.py
@@ -59,7 +59,7 @@
     ids_ref, wts_ref, grad_ref, act_ref, w_ref, skew_ref,
     hid_ref, skg_ref,
     gath, part, rxa, rxb, mida, midb, tra, trb, rgs, rotm, rotp, rotrx, pull, maskf, maskb, bys, lefts, values,
-    s_right, s_left, s_sib, r_gath, s_a, s_b, r_a, r_b, s_ma, s_mb, r_ma, r_mb,
+    s_right, s_left, s_far, s_sib, r_gath, s_a, s_b, r_a, r_b, s_ma, s_mb, r_ma, r_mb,
     s_rot, r_rot, s_pull, r_pull,
 ):
     n_dp = side * side
@@ -71,8 +71,14 @@
     half = hidden // 2
     size = skew_ref.shape[1] // PER
     per_expert = groups // 2
-    right = lax.rem(z + 1, depth) * 2 + core
-    left = lax.rem(z + depth - 1, depth) * 2 + core
+    jump = 5
+
+    def at_z(step):
+        chip = lax.rem(z + step + depth, depth)
+        return chip, chip * 2 + core
+
+    right, left = at_z(1)[1], at_z(-1)[1]
+    beyond, before = at_z(jump)[1], at_z(-jump)[1]
     sibling = z * 2 + (1 - core)
 
     def copy(src, dst, send, recv, to_dp, to_ex):
@@ -82,7 +88,7 @@
         )
 
     barrier = pltpu.get_barrier_semaphore()
-    for peer in (right, left, sibling):
+    for peer in (right, left, beyond, before, sibling):
         pl.semaphore_signal(barrier, inc=1, device_id=(dp, peer), device_id_type=MESH)
 
     def greet(step, carry):
@@ -114,7 +120,7 @@
     maskf[...] = (row_i == col_i).astype(F32)
     maskb[...] = (row_i == col_i).astype(F32).astype(BF16)
 
-    pl.semaphore_wait(barrier, n_dp - 1 + 3)
+    pl.semaphore_wait(barrier, n_dp - 1 + 5)
 
     def go_right(block):
         return copy(gath.at[block], gath.at[block], s_right.at[block // 2], r_gath.at[block], dp, right)
@@ -125,6 +131,13 @@
     def go_across(block):
         return copy(gath.at[block], gath.at[block], s_sib.at[block // 2], r_gath.at[block], dp, sibling)
 
+    def go_far(n):
+        return copy(
+            gath.at[own], gath.at[own], s_far.at[n], r_gath.at[own], dp, (beyond, before)[n]
+        )
+
+    go_far(0).start()
+    go_far(1).start()
     go_right(own).start()
     go_left(own).start()
     go_across(own).start()
@@ -208,31 +221,45 @@
     def arrived(block):
         go_right(block).wait_recv()
 
+    def get(step, on_right=False, on_left=False):
+        block = at_z(step)[1]
+        arrived(block)
+        if on_right:
+            go_right(block).start()
+        if on_left:
+            go_left(block).start()
+        go_across(block).start()
+
     arrived(sibling)
     process([z])
-
-    def ring(step, carry):
-        low = lax.rem(z - step + depth, depth)
-        high = lax.rem(z + step, depth)
-        arrived(low * 2 + core)
-        go_right(low * 2 + core).start()
-        arrived(high * 2 + core)
-
-        @pl.when(step < depth // 2 - 1)
-        def _():
-            go_left(high * 2 + core).start()
-
-        go_across(low * 2 + core).start()
-        go_across(high * 2 + core).start()
+    steps = (
+        (1, ((1, False, True), (-1, True, False))),
+        (5, ((5, True, True), (-5, True, True))),
+        (2, ((2, False, False), (-2, False, False))),
+        (4, ((4, True, False), (-6, True, False), (6, False, True), (-4, False, True))),
+        (6, ((-7, True, False), (7, False, False))),
+        (3, ((3, False, False), (-3, False, False))),
+        (7, ((8, False, False),)),
+    )
+
+    def ring(turn, carry):
+        step = 0
+        for n, (away, blocks) in enumerate(steps):
+            step = step + jnp.where(turn == n, away, 0)
+
+            @pl.when(turn == n)
+            def _():
+                for block in blocks:
+                    get(*block)
+
+        low, high = at_z(-step)[0], at_z(step)[0]
         arrived(low * 2 + 1 - core)
         arrived(high * 2 + 1 - core)
         process([low, high])
         return carry
 
-    lax.fori_loop(1, depth // 2, ring, 0)
-    far = lax.rem(z + depth // 2, depth)
-    arrived(far * 2 + core)
-    go_across(far * 2 + core).start()
+    lax.fori_loop(0, len(steps), ring, 0)
+    far = at_z(8)[0]
     arrived(far * 2 + 1 - core)
     process([far])
 
@@ -316,8 +343,8 @@
         return copy(midb.at[jy], trb.at[slot], s_mb.at[jy], r_mb.at[slot], x * side + jy, ex)
 
     def gather_both(step, carry):
-        gather_a(step, 0)
-        gather_b(step, 0)
+        gather_a(lax.rem(z // side + step + step // 2 - 2 * (step // 3), side), 0)
+        gather_b(lax.rem(y + 1 + step, side), 0)
         return carry
 
     lax.fori_loop(0, side, gather_both, 0)
@@ -338,7 +365,8 @@
     def rot_copy(group):
         return copy(rotp.at[group], rotrx.at[dp], s_rot.at[group], r_rot.at[dp], group, ex)
 
-    def grads(group, carry):
+    def grads(step, carry):
+        group = lax.rem(dp + 1 + step, groups)
         local, lanes = group // per_expert, lanes_of(group)
         square = dot(act_ref[local, :, lanes], rgs[local, :, lanes], ((0,), (0,)))
         rotp[group] = fold(square * maskf[...]).astype(BF16)
@@ -411,7 +439,9 @@
 
         lax.fori_loop(1, n_dp, tell, 0)
 
-    def write(group, carry):
+    def write(step, carry):
+        group = lax.rem(dp + groups - step, groups)
+
         @pl.when(group != dp)
         def _():
             pull_copy(group, dp).wait_recv()
@@ -421,20 +451,18 @@
 
     lax.fori_loop(0, groups, write, 0)
 
-    def left_ring(step, carry):
-        go_across(lax.rem(z + step, depth) * 2 + core).wait_send()
-
-        @pl.when(step < depth // 2)
-        def _():
-            go_right(lax.rem(z - step + depth, depth) * 2 + core).wait_send()
-
-        @pl.when(step < depth // 2 - 1)
-        def _():
-            go_left(lax.rem(z + step, depth) * 2 + core).wait_send()
-
-        return carry
-
-    lax.fori_loop(0, depth, left_ring, 0)
+    go_far(0).wait_send()
+    go_far(1).wait_send()
+    for step in (0, 5, -5, -1, 4, -6, -7):
+        go_right(at_z(step)[1]).wait_send()
+    for step in (0, 5, -5, 1, 6, -4):
+        go_left(at_z(step)[1]).wait_send()
+
+    def left_across(chip, carry):
+        go_across(chip * 2 + core).wait_send()
+        return carry
+
+    lax.fori_loop(0, depth, left_across, 0)
 
     def left_first(root, carry):
         @pl.when(root % side != y)
@@ -518,7 +546,7 @@
             pltpu.VMEM((5, wide, wide), BF16),
             pltpu.VMEM((6, size, wide), BF16),
             pltpu.VMEM((14, size, wide), F32),
-            dma((depth,)), dma((depth,)), dma((depth,)), dma((2 * depth,)),
+            dma((depth,)), dma((depth,)), dma((2,)), dma((depth,)), dma((2 * depth,)),
             dma((n_dp,)), dma((n_dp,)), dma((side, side - 1)), dma((side, side - 1)),
             dma((side,)), dma((side,)), dma((side - 1,)), dma((side - 1,)),
             dma((groups,)), dma((n_dp,)), dma((n_dp,)), dma((groups,)),

time: 101 us -> 98 us (0.970)
  the two profiles are of different devices: /device:TPU:8 before, /device:TPU:32 now
where the time goes in v3:
time: 98 us; the launch traced here: 97.7 us
  Pallas kernels  90.5 us (92%)
  local copies, waits for them, and re-layouts  6.6 us (7%)
    pallas_call x1, Pallas kernels, body(): pl.pallas_call(functools.partial(kernel, side, depth, groups), out_shape=...  90.5 us
    unnamed x11, local copies, waits for them, and re-layouts  6.56 us

profile of v3, /device:TPU:32, one launch (start us, length us, event | category | flops | bytes accessed | tf_op | source)
XLA Modules:
  0.0 97.7 jit_solution(423233400557648106)
XLA Ops:
  0.6 1.0 copy.8
  1.6 0.0 copy-start
  1.6 1.4 %copy-done = bf16[2,1536,256]{2,1,0:T(8,128)(2,1)S(1)} copy-done((bf16[2,1536,256]{2,1,0:T(8,128)(2,1)S(1)}, bf16[2,1536,256]{2,1,0:T(8,128)(2,1)}, u32[]{:S(2)}) %copy-start) | copy-done | bytes 1572888
  3.0 0.0 copy-start.1
  3.0 0.8 copy-done.1
  3.9 0.0 copy-start.2
  3.9 0.7 copy-done.2
  4.6 0.0 copy-start.3
  4.6 0.7 copy-done.3
  5.2 90.5 %shard_map.77 = (bf16[2,48,1536]{2,1,0:T(8,128)(2,1)S(1)}, f32[12,256,64]{2,1,0:T(8,128)S(1)}) custom-call(s32[8,128]{1,0:T(8,128)S(1)} %bitcast.5, f32[8,128]{1,0:T(8,128)S(1)} %bitcast.6, bf16[128,256]{1,0:T(8,128)(2,1)S(1)} %copy-done.1, bf16[2,48,1536]{2,1,0:T(8,128)(2,1)S(1)} %pad.4.act_ref, bf16[2,1536,256]{2,1,0:T(8,128)(2,1)S(1)} %copy-done, ...), custom_call_target="tpu_custom_call" | custom-call | tf_op jit(solution)/shard_map/pallas_call | solution.py:522
  95.7 0.8 copy.9
  96.6 1.1 %copy.11 = f32[2,24,64,64]{3,2,1,0:T(8,128)} copy(f32[2,24,64,64]{3,2,1,0:T(8,128)S(1)} %bitcast.4) | data formatting | bytes 1572864
  (2 shorter events, 0.0 us)
Async XLA Ops:
  1.6 1.4 %copy-start = (bf16[2,1536,256]{2,1,0:T(8,128)(2,1)S(1)}, bf16[2,1536,256]{2,1,0:T(8,128)(2,1)}, u32[]{:S(2)}) copy-start(bf16[2,1536,256]{2,1,0:T(8,128)(2,1)} %w_ref.1) | copy-start | bytes 4718596
  3.0 0.8 copy-start.1
  3.9 0.7 copy-start.2
  4.6 0.7 copy-start.3

commit v4 on v3

--- a/solution.py
+++ b/solution.py
@@ -181,6 +181,26 @@
         routed = dot(pick, rows)
         return [routed[local * HEAD : (local + 1) * HEAD] * scales[local] for local in range(2)]
 
+    chunks = half // 128
+    count = part.shape[2]
+
+    def packed(sums, row, lane):
+        def piece(value, first, rows, chunk):
+            at = lane + chunk * 128
+            return value[row + first : row + first + rows, at : at + 128]
+
+        pieces = [piece(s, 0, 32, chunk) for chunk in range(chunks) for s in sums]
+        rest = [piece(s, 32, 8, chunk) for s in sums for chunk in range(chunks)]
+        for first in range(0, len(rest), 4):
+            tile = rest[first]
+            for k, other in enumerate(rest[first + 1 : first + 4]):
+                tile = tile + pltpu.roll(other, 2 * k + 2, 0)
+            pieces.append(tile)
+        spare = count - sum(p.shape[0] for p in pieces)
+        if spare:
+            pieces.append(jnp.zeros((spare, 128), F32))
+        return jnp.concatenate(pieces, axis=0)
+
     def process(roots):
         found = [rows_of(root) for root in roots]
         sums = []
@@ -189,13 +209,7 @@
             sums.append(dot(lhs, w_ref[local], ((1,), (1,))))
         for n, root in enumerate(roots):
             for which in range(2):
-                part[root, which] = jnp.concatenate(
-                    [
-                        s[n * HEAD : (n + 1) * HEAD, which * half : (which + 1) * half]
-                        for s in sums
-                    ],
-                    axis=0,
-                ).astype(BF16)
+                part[root, which] = packed(sums, n * HEAD, which * half).astype(BF16)
             jx, jy = root // side, root % side
 
             @pl.when(jy != y)
@@ -355,9 +369,18 @@
             copy(mid.at[0], tr.at[slot], s_m.at[0], r_m.at[slot], dp, ex).wait_recv()
             total = total + tr[slot].astype(F32)
         for local in range(2):
-            rgs[local, :, which * half : (which + 1) * half] = jnp.concatenate(
-                [total[local * HEAD : (local + 1) * HEAD], jnp.zeros((DEEP - HEAD, half), F32)], axis=0
-            ).astype(BF16)
+            for chunk in range(chunks):
+                at = local * chunks + chunk
+                start = 64 * chunks + at // 4 * 8
+                tile = total[start : start + 8]
+                if at % 4:
+                    tile = pltpu.roll(tile, 8 - at % 4 * 2, 0)
+                tile = jnp.where(lax.broadcasted_iota(jnp.int32, (8, 128), 0) < 2, tile, 0.0)
+                start = chunk * 64 + local * 32
+                lane = which * half + chunk * 128
+                rgs[local, :, lane : lane + 128] = jnp.concatenate(
+                    [total[start : start + 32], tile, jnp.zeros((DEEP - HEAD, 128), F32)], axis=0
+                ).astype(BF16)
 
     def lanes_of(group):
         return pl.ds(pl.multiple_of((group % per_expert) * PER * size, PER * size), PER * size)
@@ -516,6 +539,8 @@
     n_dp = side * side
     half = hidden // 2
     wide = PER * size
+    chunks = half // 128
+    packed = -(-(64 * chunks + (2 * chunks + 3) // 4 * 8) // 16) * 16
     act = jnp.pad(hidden_act, ((0, 0), (0, DEEP - slots_here), (0, 0)))
     vmem = pl.BlockSpec(memory_space=pltpu.VMEM)
     dma = pltpu.SemaphoreType.DMA
@@ -529,13 +554,13 @@
         out_specs=(vmem, vmem),
         scratch_shapes=[
             pltpu.VMEM((2 * depth, tokens + 16, feat), BF16),
-            pltpu.VMEM((n_dp, 2, 2 * HEAD, half), BF16),
-            pltpu.VMEM((side, side - 1, 2 * HEAD, half), BF16),
-            pltpu.VMEM((side, side - 1, 2 * HEAD, half), BF16),
-            pltpu.VMEM((side, 2 * HEAD, half), BF16),
-            pltpu.VMEM((side, 2 * HEAD, half), BF16),
-            pltpu.VMEM((side - 1, 2 * HEAD, half), BF16),
-            pltpu.VMEM((side - 1, 2 * HEAD, half), BF16),
+            pltpu.VMEM((n_dp, 2, packed, 128), BF16),
+            pltpu.VMEM((side, side - 1, packed, 128), BF16),
+            pltpu.VMEM((side, side - 1, packed, 128), BF16),
+            pltpu.VMEM((side, packed, 128), BF16),
+            pltpu.VMEM((side, packed, 128), BF16),
+            pltpu.VMEM((side - 1, packed, 128), BF16),
+            pltpu.VMEM((side - 1, packed, 128), BF16),
             pltpu.VMEM((local, DEEP, hidden), BF16),
             pltpu.VMEM((groups, wide, wide), BF16),
             pltpu.VMEM((groups, size, wide), BF16),

time: 98 us -> 97.3 us (level)
  no operation moved by 1% of the time
where the time goes in v4:
time: 97.3 us; the launch traced here: 97 us
  Pallas kernels  89.7 us (92%)
  local copies, waits for them, and re-layouts  6.6 us (7%)
    pallas_call x1, Pallas kernels, body(): pl.pallas_call(functools.partial(kernel, side, depth, groups), out_shape=...  89.7 us
    unnamed x11, local copies, waits for them, and re-layouts  6.56 us

profile of v4, /device:TPU:32, one launch (start us, length us, event | category | flops | bytes accessed | tf_op | source)
XLA Modules:
  0.0 97.0 jit_solution(17413352342753033224)
XLA Ops:
  0.6 1.0 copy.8
  1.6 0.0 copy-start
  1.6 1.4 %copy-done = bf16[2,1536,256]{2,1,0:T(8,128)(2,1)S(1)} copy-done((bf16[2,1536,256]{2,1,0:T(8,128)(2,1)S(1)}, bf16[2,1536,256]{2,1,0:T(8,128)(2,1)}, u32[]{:S(2)}) %copy-start) | copy-done | bytes 1572888
  3.0 0.0 copy-start.1
  3.0 0.8 copy-done.1
  3.9 0.0 copy-start.2
  3.9 0.7 copy-done.2
  4.6 0.0 copy-start.3
  4.6 0.7 copy-done.3
  5.2 89.7 %shard_map.77 = (bf16[2,48,1536]{2,1,0:T(8,128)(2,1)S(1)}, f32[12,256,64]{2,1,0:T(8,128)S(1)}) custom-call(s32[8,128]{1,0:T(8,128)S(1)} %bitcast.5, f32[8,128]{1,0:T(8,128)S(1)} %bitcast.6, bf16[128,256]{1,0:T(8,128)(2,1)S(1)} %copy-done.1, bf16[2,48,1536]{2,1,0:T(8,128)(2,1)S(1)} %pad.4.act_ref, bf16[2,1536,256]{2,1,0:T(8,128)(2,1)S(1)} %copy-done, ...), custom_call_target="tpu_custom_call" | custom-call | tf_op jit(solution)/shard_map/pallas_call | solution.py:547
  95.0 0.8 copy.9
  95.9 1.1 %copy.11 = f32[2,24,64,64]{3,2,1,0:T(8,128)} copy(f32[2,24,64,64]{3,2,1,0:T(8,128)S(1)} %bitcast.4) | data formatting | bytes 1572864
  (2 shorter events, 0.0 us)
Async XLA Ops:
  1.6 1.4 %copy-start = (bf16[2,1536,256]{2,1,0:T(8,128)(2,1)S(1)}, bf16[2,1536,256]{2,1,0:T(8,128)(2,1)}, u32[]{:S(2)}) copy-start(bf16[2,1536,256]{2,1,0:T(8,128)(2,1)} %w_ref.1) | copy-start | bytes 4718596
  3.0 0.8 copy-start.1
  3.9 0.7 copy-start.2
  4.6 0.7 copy-start.3

commit v5 on v4

--- a/solution.py
+++ b/solution.py
@@ -409,6 +409,11 @@
 
     lax.fori_loop(0, groups, hide, 0)
 
+    def above(sign):
+        shape = (size, PER * size // 2)
+        row = lax.broadcasted_iota(jnp.int32, shape, 0)
+        return sign * (lax.rem(lax.broadcasted_iota(jnp.int32, shape, 1), size) - row) > 0
+
     def pull_copy(owner, peer):
         return copy(pull.at[owner], pull.at[owner], s_pull.at[peer], r_pull.at[owner], peer, ex)
 
@@ -454,7 +459,11 @@
         (back,) = put(13, change_b, bys[4])
         result = front + four_change + back
         square = spread(result, maskf[...])
-        pull[dp] = fold(square.T - square).astype(BF16)
+        slab = fold(square.T - square)
+        wide = PER * size // 2
+        pull[dp] = jnp.where(
+            above(1), slab[:, :wide], jnp.where(above(-1), slab[:, wide:], 0.0)
+        ).astype(BF16)
 
         def tell(step, carry):
             pull_copy(dp, lax.rem(dp + step, n_dp)).start()
@@ -469,7 +478,11 @@
         def _():
             pull_copy(group, dp).wait_recv()
 
-        skg_ref[group] = -(pull[group].astype(F32).T)
+        given = pull[group].astype(F32)
+        for n, sign in enumerate((1, -1)):
+            part_of = jnp.where(above(sign), given, 0.0)
+            stacked = jnp.concatenate([part_of[:, :size], part_of[:, size:]], axis=0)
+            skg_ref[group, n * 2 * size : (n + 1) * 2 * size, :] = stacked - part_of.T
         return carry
 
     lax.fori_loop(0, groups, write, 0)
@@ -565,7 +578,7 @@
             pltpu.VMEM((groups, wide, wide), BF16),
             pltpu.VMEM((groups, size, wide), BF16),
             pltpu.VMEM((n_dp, size, wide), BF16),
-            pltpu.VMEM((groups, size, wide), BF16),
+            pltpu.VMEM((groups, size, wide // 2), BF16),
             pltpu.VMEM((wide, wide), F32),
             pltpu.VMEM((wide, wide), BF16),
             pltpu.VMEM((5, wide, wide), BF16),

time: 97.3 us -> 95.8 us (0.985)
  Pallas kernels: 89.7 us -> 88.2 us
    pallas_call x1, Pallas kernels: 89.7 us -> 88.2 us  [body(): pl.pallas_call(functools.partial(kernel, side, depth, groups), out_shape=...]
where the time goes in v5:
time: 95.8 us; the launch traced here: 95.5 us
  Pallas kernels  88.2 us (92%)
  local copies, waits for them, and re-layouts  6.6 us (7%)
    pallas_call x1, Pallas kernels, body(): pl.pallas_call(functools.partial(kernel, side, depth, groups), out_shape=...  88.2 us
    unnamed x11, local copies, waits for them, and re-layouts  6.56 us

profile of v5, /device:TPU:32, one launch (start us, length us, event | category | flops | bytes accessed | tf_op | source)
XLA Modules:
  0.0 95.5 jit_solution(5582426612450059945)
XLA Ops:
  0.6 1.0 %copy.8 = bf16[2,34,1536]{2,1,0:T(8,128)(2,1)S(1)} copy(bf16[2,34,1536]{2,0,1:T(2,128)(2,1)} %param.9) | data formatting | bytes 417792 | tf_op args[3]
  1.6 0.0 copy-start
  1.6 1.4 %copy-done = bf16[2,1536,256]{2,1,0:T(8,128)(2,1)S(1)} copy-done((bf16[2,1536,256]{2,1,0:T(8,128)(2,1)S(1)}, bf16[2,1536,256]{2,1,0:T(8,128)(2,1)}, u32[]{:S(2)}) %copy-start) | copy-done | bytes 1572888
  3.0 0.0 copy-start.1
  3.0 0.8 copy-done.1
  3.9 0.0 copy-start.2
  3.9 0.7 copy-done.2
  4.6 0.0 copy-start.3
  4.6 0.7 copy-done.3
  5.2 88.2 %shard_map.77 = (bf16[2,48,1536]{2,1,0:T(8,128)(2,1)S(1)}, f32[12,256,64]{2,1,0:T(8,128)S(1)}) custom-call(s32[8,128]{1,0:T(8,128)S(1)} %bitcast.5, f32[8,128]{1,0:T(8,128)S(1)} %bitcast.6, bf16[128,256]{1,0:T(8,128)(2,1)S(1)} %copy-done.1, bf16[2,48,1536]{2,1,0:T(8,128)(2,1)S(1)} %pad.4.act_ref, bf16[2,1536,256]{2,1,0:T(8,128)(2,1)S(1)} %copy-done, ...), custom_call_target="tpu_custom_call" | custom-call | tf_op jit(solution)/shard_map/pallas_call | solution.py:560
  93.5 0.8 copy.9
  94.3 1.1 %copy.11 = f32[2,24,64,64]{3,2,1,0:T(8,128)} copy(f32[2,24,64,64]{3,2,1,0:T(8,128)S(1)} %bitcast.4) | data formatting | bytes 1572864
  (2 shorter events, 0.0 us)
Async XLA Ops:
  1.6 1.4 %copy-start = (bf16[2,1536,256]{2,1,0:T(8,128)(2,1)S(1)}, bf16[2,1536,256]{2,1,0:T(8,128)(2,1)}, u32[]{:S(2)}) copy-start(bf16[2,1536,256]{2,1,0:T(8,128)(2,1)} %w_ref.1) | copy-start | bytes 4718596
  3.0 0.8 copy-start.1
  3.9 0.7 copy-start.2
  4.6 0.7 copy-start.3
